TPU v7x, 32 devices: a whole 2x2x4 slice. The times are simulated.
32 devices in a mesh: row: 8 (over z, core), col: 4 (over y, x).
Axes of the slice: x: 2, y: 2, z: 4, core: 2. Of those that a mesh axis runs over, the one named last changes fastest.
Arguments:
- design: bfloat16 [1024, 26624], P('row', 'col'), may hold values from -0.5 to 0.5
- group_ids: int32 [1024], replicated, may hold values from 0 to 3, never falling along the last dimension, each value on 1 to 512 neighbouring positions
- filter_zeros: float32 [2], replicated, may hold values from 0.3 to 1, as said below
- filter_poles: float32 [2], replicated, may hold values from 0.8 to 1, as said below
Outputs:
- normal: float32 [26624, 26624], P('row', 'col')
Inputs may be any that keep to these rules, and one draw needn't show every extreme that they name: `group_ids`: epochs in time order; group numbers never fall along time and each group is 1 to 512 epochs long. `filter_zeros`: one zero lies in [0.3, 0.7], the other within 0.2 / 1024 below 1. `filter_poles`: one pole lies in [0.8, 0.95], the other within 2 / 1024 below 1.
All inputs are finite; a program needn't handle non-finite values.
Results may differ from a plain program's by a relative error of at most 0.0022.
Values may be sent and summed in bfloat16 or wider, within the bound.
No kernel may reach another device: no remote copies, remote signals or barrier semaphores. Data moves between devices by JAX's collectives and lax.ppermute only.
A program may use at most 192 MiB of HBM per device.

v0:
```python
import functools

import jax
import jax.numpy as jnp
from jax import lax
from jax.experimental import pallas as pl
from jax.experimental.pallas import tpu as pltpu
from jax.sharding import PartitionSpec as P

VMEM_BYTES = 56 * 1024 * 1024
COLUMN_UNITS = (8, 5)


def block_matrices(group_ids, filter_zeros, filter_poles, rows):
    p, z = filter_poles, filter_zeros
    share = jnp.stack(
        [
            (p[0] - z[0]) * (p[0] - z[1]) / (p[0] - p[1]),
            (p[1] - z[0]) * (p[1] - z[1]) / (p[1] - p[0]),
        ]
    )
    g = group_ids.reshape(rows, -1)
    length = g.shape[1]
    i = jnp.arange(length, dtype=jnp.int32)
    powers = p[:, None] ** jnp.arange(length + 1, dtype=jnp.float32)[None, :]
    lag = i[:, None] - i[None, :]
    ahead = jnp.maximum(lag - 1, 0).astype(jnp.float32)
    response = jnp.where(lag == 0, 1.0, share[0] * p[0] ** ahead + share[1] * p[1] ** ahead)
    same = (g[:, :, None] == g[:, None, :]) & (lag >= 0)
    inside = jnp.where(same, response, 0.0)
    left = (length - 1 - i).astype(jnp.float32)
    ends = share[:, None] * p[:, None] ** left[None, :]
    ends = jnp.where((g == g[:, -1:])[:, None, :], ends[None], 0.0)
    matrix = jnp.concatenate([inside, jnp.pad(ends, ((0, 0), (0, 14), (0, 0)))], axis=1)
    high = lax.reduce_precision(matrix, 8, 7)
    matrix = jnp.concatenate([high, matrix - high], axis=2).astype(jnp.bfloat16)
    before = jnp.concatenate([jnp.full((1,), -1, jnp.int32), g[:-1, -1]])
    reached = (g == before[:, None]).astype(jnp.float32)
    gains = reached[:, :, None] * powers[:, :length].T[None]
    keep = reached[:, -1:, None] * powers[:, length][None, None, :]
    gains = jnp.concatenate([gains, jnp.broadcast_to(keep, gains.shape)], axis=2)
    return matrix, jnp.pad(gains, ((0, 0), (0, 0), (0, 4)))


def whiten_blocks(rows, blocks, matrix, gains, put):
    one = two = None
    for b in range(rows):
        block = blocks(b)
        length = block.shape[0]
        full = jnp.dot(
            matrix[b], jnp.concatenate([block, block], axis=0), preferred_element_type=jnp.float32
        )
        values = full[:length]
        ends = full[length : length + 1], full[length + 1 : length + 2]
        if b > 0:
            values = values + gains[b, :, 0:1] * one + gains[b, :, 1:2] * two
            ends = ends[0] + gains[b, 0:1, 2:3] * one, ends[1] + gains[b, 0:1, 3:4] * two
        one, two = ends
        put(b, values.astype(jnp.bfloat16))


def tile_of(width):
    return width if width <= 1024 else next(t for t in (1024, 896, 768, 640, 512, 256, 128) if width % t == 0)


def whiten_columns_kernel(rows, core, raw, matrix, gains, panel):
    length = raw.shape[0] // rows

    def put(b, values):
        panel[b * length : (b + 1) * length, :] = values

    whiten_blocks(rows, lambda b: raw[b * length : (b + 1) * length, :], matrix, gains, put)


def whiten_columns(core, raw, width, matrix, gains):
    epochs, rows, tile = raw.shape[0], matrix.shape[0], tile_of(width)
    tiles = width // tile
    whole = lambda a: pl.BlockSpec(a.shape, lambda i, s: (0, 0, 0))
    return pl.pallas_call(
        functools.partial(whiten_columns_kernel, rows),
        grid_spec=pltpu.PrefetchScalarGridSpec(
            num_scalar_prefetch=1,
            grid=(tiles,),
            in_specs=[pl.BlockSpec((epochs, tile), lambda i, s: (0, s[0] * tiles + i)), whole(matrix), whole(gains)],
            out_specs=pl.BlockSpec((epochs, tile), lambda i, s: (0, i)),
        ),
        out_shape=jax.ShapeDtypeStruct((epochs, width), jnp.bfloat16),
        compiler_params=pltpu.CompilerParams(vmem_limit_bytes=VMEM_BYTES),
        cost_estimate=pl.CostEstimate(
            flops=8 * 144 * 256 * rows * width, bytes_accessed=4 * epochs * width, transcendentals=0
        ),
        name="whiten_columns",
    )(core, raw, matrix, gains)


def whiten_rows_kernel(rows, place, raw, matrix, gains, turned, held):
    core, chip = place[0], place[1]
    chips, length = rows // 2, raw.shape[1]

    def blocks(b):
        return raw[jnp.bitwise_xor(core, b % 2) * chips + jnp.bitwise_xor(chip, b // 2)]

    def put(b, values):
        held[b * length : (b + 1) * length, :] = values

    whiten_blocks(rows, blocks, matrix, gains, put)
    turned[...] = held[...].T


def whiten_rows(place, raw, width, matrix, gains):
    rows, length, tile = matrix.shape[0], raw.shape[1], tile_of(width)
    epochs = rows * length
    whole = lambda a: pl.BlockSpec(a.shape, lambda i, s: (0, 0, 0))
    return pl.pallas_call(
        functools.partial(whiten_rows_kernel, rows),
        grid_spec=pltpu.PrefetchScalarGridSpec(
            num_scalar_prefetch=1,
            grid=(width // tile,),
            in_specs=[pl.BlockSpec((rows, length, tile), lambda i, s: (0, 0, i)), whole(matrix), whole(gains)],
            out_specs=pl.BlockSpec((tile, epochs), lambda i, s: (i, 0)),
            scratch_shapes=[pltpu.VMEM((epochs, tile), jnp.bfloat16)],
        ),
        out_shape=jax.ShapeDtypeStruct((width, epochs), jnp.bfloat16),
        compiler_params=pltpu.CompilerParams(vmem_limit_bytes=VMEM_BYTES),
        cost_estimate=pl.CostEstimate(
            flops=8 * 144 * 256 * rows * width, bytes_accessed=4 * epochs * width, transcendentals=0
        ),
        name="whiten_rows",
    )(place, raw, matrix, gains)


def product_kernel(parts, wides, pairs, sub, chained, place, *refs):
    n, m = len(parts), len(wides)
    piece_refs, column_refs = refs[:n], refs[n : n + m]
    out = refs[n + m + chained]
    rest = refs[n + m + chained + 1 :]
    held, wide, stage = rest[:n], rest[n : n + m], rest[n + m]
    piece_sem, column_sem, stage_sem = rest[n + m + 1 :]
    loads = {}
    for i, j in pairs:
        if ("piece", i) not in loads:
            loads["piece", i] = pltpu.make_async_copy(piece_refs[i], held[i], piece_sem.at[i])
        if ("wide", j) not in loads:
            loads["wide", j] = pltpu.make_async_copy(column_refs[j], wide[j], column_sem.at[j])
    for copy in loads.values():
        copy.start()
    slots = stage.shape[0]
    flying = [None] * slots
    turn = 0
    for i, j in pairs:
        for key in (("piece", i), ("wide", j)):
            if key in loads:
                loads.pop(key).wait()
        own, start, width = wides[j]
        home = place[0] if own else 1 - place[0]
        column = pl.multiple_of(home * sub + start, 128)
        for at, size, entry in parts[i]:
            slot = turn % slots
            if flying[slot] is not None:
                flying[slot].wait()
            stage[slot, :size, :width] = jnp.dot(
                held[i][at : at + size, :], wide[j][...], preferred_element_type=jnp.float32
            )
            flying[slot] = pltpu.make_async_copy(
                stage.at[slot, pl.ds(0, size), pl.ds(0, width)],
                out.at[pl.ds(pl.multiple_of(place[entry], 64), size), pl.ds(column, width)],
                stage_sem.at[slot],
            )
            flying[slot].start()
            turn += 1
    for copy in flying:
        if copy is not None:
            copy.wait()


def product(place, pieces, columns, pairs, out, shape, sub):
    parts = [segments for segments, _ in pieces]
    heights = [p.shape[0] for _, p in pieces]
    wides = [(own, s, c.shape[1]) for own, s, c in columns]
    epochs = columns[0][2].shape[0]
    done = sum(heights[i] * wides[j][2] for i, j in pairs)
    chained = int(out is not None)
    anywhere = pl.BlockSpec(memory_space=pl.ANY)
    args = [p for _, p in pieces] + [c for _, _, c in columns] + ([out] if chained else [])
    tall, broad = max(size for p in parts for _, size, _ in p), max(w for _, _, w in wides)
    return pl.pallas_call(
        functools.partial(product_kernel, parts, wides, pairs, sub, chained),
        grid_spec=pltpu.PrefetchScalarGridSpec(
            num_scalar_prefetch=1,
            grid=(),
            in_specs=[anywhere] * len(args),
            out_specs=anywhere,
            scratch_shapes=[pltpu.VMEM((h, epochs), jnp.bfloat16) for h in heights]
            + [pltpu.VMEM((epochs, w), jnp.bfloat16) for _, _, w in wides]
            + [
                pltpu.VMEM((3, tall, broad), jnp.float32),
                pltpu.SemaphoreType.DMA((len(heights),)),
                pltpu.SemaphoreType.DMA((len(wides),)),
                pltpu.SemaphoreType.DMA((3,)),
            ],
        ),
        out_shape=jax.ShapeDtypeStruct(shape, jnp.float32),
        input_output_aliases={len(args): 0} if chained else {},
        compiler_params=pltpu.CompilerParams(vmem_limit_bytes=VMEM_BYTES),
        cost_estimate=pl.CostEstimate(
            flops=2 * epochs * done,
            bytes_accessed=4 * done + 2 * epochs * (sum(heights) + sum(w for _, _, w in wides)),
            transcendentals=0,
        ),
        name="product",
    )(place, *args)


def tied(values, others):
    return lax.optimization_barrier((values, others))[0]


def swapped(value, axis, distance):
    return lax.ppermute(value, axis, [(i, i ^ distance) for i in range(lax.axis_size(axis))])


def share_start(index, share, sub):
    return jnp.minimum(index * share, sub - share)


def row_share(design, share):
    col_count, chips = lax.axis_size("col"), lax.axis_size("row") // 2
    row, col = lax.axis_index("row"), lax.axis_index("col")
    core, chip = lax.rem(row, 2), row // 2
    sub = design.shape[1] // 2

    def given(d):
        start = share_start(jnp.bitwise_xor(col, d), share, sub)
        return jnp.concatenate(
            [lax.dynamic_slice_in_dim(design, h * sub + start, share, 1) for h in range(2)], axis=1
        )

    panels = jnp.stack([given(0)] + [swapped(given(d), "col", d) for d in range(1, col_count)])
    held = lambda e: lax.dynamic_index_in_dim(panels, jnp.bitwise_xor(jnp.bitwise_xor(chip, e), col), 0, False)
    mine = jnp.stack([held(0)] + [swapped(held(e), "row", 2 * e) for e in range(1, chips)])
    keep = lax.dynamic_slice_in_dim(mine, core * share, share, 2)
    give = lax.dynamic_slice_in_dim(mine, (1 - core) * share, share, 2)
    return jnp.concatenate([keep, swapped(give, "row", 1)], axis=0)


def all_shares(part, first, order):
    held, away, steps = part, [0], [([order[0]], first)]
    for k, d in enumerate(order):
        new, far = (first if k == 0 else swapped(held, "col", d)), [a ^ d for a in away]
        if k > 0:
            steps.append((far, new))
        if k + 1 < len(order):
            held, away = jnp.concatenate([held, new], axis=0), away + far
    return steps


def local(design, group_ids, filter_zeros, filter_poles):
    row_count, col_count = lax.axis_size("row"), lax.axis_size("col")
    row, col = lax.axis_index("row"), lax.axis_index("col")
    core = lax.rem(row, 2)
    panel_width = design.shape[1]
    sub = panel_width // 2
    unit = sub // 13
    share = -(-sub // (128 * col_count)) * 128
    distances = [2**k for k in range((col_count - 1).bit_length())]
    starts = [share_start(jnp.bitwise_xor(col, d), share, sub) + p * (share // 2) for p in range(2) for d in range(col_count)]
    place = jnp.stack([core, row // 2] + starts).astype(jnp.int32)
    entry = lambda distance, part: 2 + part * col_count + distance
    matrix, gains = block_matrices(group_ids, filter_zeros, filter_poles, row_count)

    core_arg = core.reshape(1)
    raws, at = [], 0
    for units in COLUMN_UNITS:
        end = at + units * unit
        mine = jnp.concatenate([design[:, at:end], design[:, sub + at : sub + end]], axis=1)
        if raws:
            mine = tied(mine, matrix)
        raws.append((at, lax.all_gather(mine, "row", axis=0, tiled=True)))
        at = end

    turned = whiten_rows(place, row_share(design, share), share, matrix, gains)
    half = share // 2
    orders = [distances[p:] + distances[:p] for p in range(2)]
    parts = [turned[p * half : (p + 1) * half] for p in range(2)]
    firsts = [swapped(parts[p], "col", orders[p][0]) for p in range(2)]

    def columns_of(k, after):
        start, raw = raws[k]
        mine = whiten_columns(core_arg, tied(raw, after), COLUMN_UNITS[k] * unit, matrix, gains)
        return (True, start, mine), (False, start, swapped(mine, "row", 1))

    shape = (sub, panel_width)
    own, others = columns_of(0, turned)
    whole = ([(0, half, entry(0, 0)), (half, half, entry(0, 1))], turned)
    out = product(place, [whole], [own], [(0, 0)], None, shape, sub)
    out, firsts = lax.optimization_barrier((out, firsts))
    steps = [all_shares(parts[p], firsts[p], orders[p]) for p in range(2)]
    groups = [[whole]]
    for k in range(len(distances)):
        group = []
        for p in range(2):
            far, new = steps[p][k]
            group.append(([(s * half, half, entry(d, p)) for s, d in enumerate(far)], new))
        groups.append(group)

    early = [piece for group in groups[:-1] for piece in group]
    pairs = [(0, 1)] + [(i, j) for i in range(1, len(early)) for j in range(2)]
    out = product(place, early, [own, others], pairs, out, shape, sub)
    out, raw = lax.optimization_barrier((out, raws[1][1]))
    raws[1] = (raws[1][0], raw)
    more = columns_of(1, own[2])
    late = groups[-1]
    out, mine = lax.optimization_barrier((out, more[0][2]))
    more = ((True, more[0][1], mine), more[1])
    out = product(place, late, [own, others], [(i, j) for j in range(2) for i in range(len(late))], out, shape, sub)
    every = early + late
    return product(place, every, more, [(i, j) for j in range(2) for i in range(len(every))], out, shape, sub)


def solution(mesh):
    return jax.shard_map(
        local,
        mesh=mesh,
        in_specs=(P("row", "col"), P(), P(), P()),
        out_specs=P("row", "col"),
        check_vma=False,
    )
```

profile of v0, /device:TPU:8, one launch (start us, length us, event | category | flops | bytes accessed | tf_op | source)
XLA Modules:
  0.0 274.1 jit_solution(6064455590579441150)
XLA Ops:
  11.5 1.5 collective-permute-start
  13.8 1.5 collective-permute-start.1
  24.4 1.4 add_select_fusion
  28.7 12.1 %collective-permute-done.2 = bf16[128,1792]{1,0:T(8,128)(2,1)S(1)} collective-permute-done((bf16[128,1792]{1,0:T(8,128)(2,1)S(1)}, bf16[128,1792]{1,0:T(8,128)(2,1)S(1)}, u32[]{:S(2)}, u32[]{:S(2)}) %collective-permute-start.2) | collective-permute-done | bytes 458784 | tf_op jit(solution)/shard_map/ppermute | solution.py:219
  41.7 2.6 collective-permute-start.4
  44.8 36.2 %collective-permute-done.3 = bf16[128,1792]{1,0:T(8,128)(2,1)S(1)} collective-permute-done((bf16[128,1792]{1,0:T(8,128)(2,1)S(1)}, bf16[128,1792]{1,0:T(8,128)(2,1)S(1)}, u32[]{:S(2)}, u32[]{:S(2)}) %collective-permute-start.3) | collective-permute-done | bytes 458784 | tf_op jit(solution)/shard_map/ppermute | solution.py:219
  81.0 4.7 %collective-permute-done.4 = bf16[128,1792]{1,0:T(8,128)(2,1)S(1)} collective-permute-done((bf16[128,1792]{1,0:T(8,128)(2,1)S(1)}, bf16[128,1792]{1,0:T(8,128)(2,1)S(1)}, u32[]{:S(2)}, u32[]{:S(2)}) %collective-permute-start.4) | collective-permute-done | bytes 458784 | tf_op jit(solution)/shard_map/ppermute | solution.py:219
  85.7 40.8 %collective-permute-done.5 = bf16[128,1792]{1,0:T(8,128)(2,1)S(1)} collective-permute-done((bf16[128,1792]{1,0:T(8,128)(2,1)S(1)}, bf16[128,1792]{1,0:T(8,128)(2,1)S(1)}, u32[]{:S(2)}, u32[]{:S(2)}) %collective-permute-start.5) | collective-permute-done | bytes 458784 | tf_op jit(solution)/shard_map/ppermute | solution.py:219
  129.6 1.4 pad_maximum_fusion.2.raw
  131.0 4.8 %whiten_rows.1.refs_0_ = bf16[896,1024]{1,0:T(8,128)(2,1)} custom-call(s32[10]{0:T(128)} %stack.80.place, bf16[8,128,896]{2,1,0:T(8,128)(2,1)} %pad_maximum_fusion.2.raw, bf16[8,144,256]{2,1,0:T(8,128)(2,1)} %pad_maximum_fusion.7.matrix, f32[8,128,8]{2,1,0:T(8,128)} %pad.9.gains), custom_call_target="tpu_custom_call" | custom-call | flops 2113929216 | bytes 3670016 | tf_op jit(solution)/shard_map/whiten_rows/pallas_call | solution.py:114
  135.8 5.5 %whiten_columns.2.refs_1_.refs_3_.refs_2_ = bf16[1024,2048]{1,0:T(8,128)(2,1)} custom-call(s32[1]{0:T(128)} %bitcast.core, bf16[1024,4096]{1,0:T(8,128)(2,1)} %all-gather.3.cloned.1.call-done.raw, bf16[8,144,256]{2,1,0:T(8,128)(2,1)} %pad_maximum_fusion.7.matrix, f32[8,128,8]{2,1,0:T(8,128)} %pad.9.gains), custom_call_target="tpu_custom_call" | custom-call | flops 4831838208 | bytes 8388608 | tf_op jit(solution)/shard_map/whiten_columns/pallas_call | solution.py:79
  144.2 9.4 %product.4.refs_5_ = f32[3328,6656]{1,0:T(8,128)} custom-call(s32[10]{0:T(128)} %stack.80.place, bf16[896,1024]{1,0:T(8,128)(2,1)} %whiten_rows.1.refs_0_, bf16[1024,2048]{1,0:T(8,128)(2,1)} %whiten_columns.2.refs_1_.refs_3_.refs_2_), custom_call_target="tpu_custom_call" | custom-call | flops 3758096384 | bytes 13369344 | tf_op jit(solution)/shard_map/product/pallas_call | solution.py:186
  153.5 11.7 %collective-permute-done.7.refs_1_ = bf16[448,1024]{1,0:T(8,128)(2,1)S(1)} collective-permute-done((bf16[448,1024]{1,0:T(8,128)(2,1)S(1)}, bf16[448,1024]{1,0:T(8,128)(2,1)S(1)}, u32[]{:S(2)}, u32[]{:S(2)}) %collective-permute-start.7) | collective-permute-done | bytes 917536 | tf_op jit(solution)/shard_map/ppermute | solution.py:219
  165.9 2.9 %pad_maximum_fusion.4 = bf16[896,1024]{1,0:T(8,128)(2,1)} fusion(bf16[448,1024]{1,0:T(8,128)(2,1)S(1)} %collective-permute-done.8.refs_2_, bf16[448,1024]{1,0:T(8,128)(2,1)} %get-tuple-element.25), kind=kLoop, calls=%fused_computation.4 | loop fusion | flops 3670016 | bytes 3670016 | tf_op jit(solution)/shard_map/concatenate | solution.py:253
  168.8 1.3 collective-permute-start.10
  170.2 1.4 pad_maximum_fusion.3
  172.2 2.0 copy-done.1
  174.2 17.6 %product.5.refs_4_ = f32[3328,6656]{1,0:T(8,128)} custom-call(s32[10]{0:T(128)} %stack.80.place, bf16[896,1024]{1,0:T(8,128)(2,1)} %whiten_rows.1.refs_0_, bf16[448,1024]{1,0:T(8,128)(2,1)} %copy-done.2, bf16[448,1024]{1,0:T(8,128)(2,1)} %copy-done.3, bf16[1024,2048]{1,0:T(8,128)(2,1)} %whiten_columns.2.refs_1_.refs_3_.refs_2_, ...), custom_call_target="tpu_custom_call", output_to_operand_aliasing={{}: (6, {})} | custom-call | flops 11274289152 | bytes 34078720 | tf_op jit(solution)/shard_map/product/pallas_call | solution.py:186
  191.8 4.5 %whiten_columns.3.refs_5_ = bf16[1024,1280]{1,0:T(8,128)(2,1)} custom-call(s32[1]{0:T(128)} %bitcast.core, bf16[1024,2560]{1,0:T(8,128)(2,1)} %all-gather.5.cloned.1.call-done.raw, bf16[8,144,256]{2,1,0:T(8,128)(2,1)} %pad_maximum_fusion.7.matrix, f32[8,128,8]{2,1,0:T(8,128)} %pad.9.gains), custom_call_target="tpu_custom_call" | custom-call | flops 3019898880 | bytes 5242880 | tf_op jit(solution)/shard_map/whiten_columns/pallas_call | solution.py:79
  196.5 13.9 %collective-permute-done.10.refs_1_.refs_4_ = bf16[896,1024]{1,0:T(8,128)(2,1)} collective-permute-done((bf16[896,1024]{1,0:T(8,128)(2,1)}, bf16[896,1024]{1,0:T(8,128)(2,1)}, u32[]{:S(2)}, u32[]{:S(2)}) %collective-permute-start.10) | collective-permute-done | bytes 1835040 | tf_op jit(solution)/shard_map/ppermute | solution.py:219
  210.3 2.3 collective-permute-done.9.refs_0_.refs_3_
  213.9 21.7 %product.6.refs_7_ = f32[3328,6656]{1,0:T(8,128)} custom-call(s32[10]{0:T(128)} %stack.80.place, bf16[896,1024]{1,0:T(8,128)(2,1)} %copy-done.5, bf16[896,1024]{1,0:T(8,128)(2,1)} %collective-permute-done.10.refs_1_.refs_4_, bf16[1024,2048]{1,0:T(8,128)(2,1)} %whiten_columns.2.refs_1_.refs_3_.refs_2_, ...), custom_call_target="tpu_custom_call", output_to_operand_aliasing={{}: (5, {})} | custom-call | flops 15032385536 | bytes 41418752 | tf_op jit(solution)/shard_map/product/pallas_call | solution.py:186
  235.6 1.5 copy-done.6
  237.1 29.9 %product.7 = f32[3328,6656]{1,0:T(8,128)} custom-call(s32[10]{0:T(128)} %stack.80.place, bf16[896,1024]{1,0:T(8,128)(2,1)} %whiten_rows.1.refs_0_, bf16[448,1024]{1,0:T(8,128)(2,1)} %copy-done.2, bf16[448,1024]{1,0:T(8,128)(2,1)} %copy-done.3, bf16[896,1024]{1,0:T(8,128)(2,1)} %copy-done.5, ...), custom_call_target="tpu_custom_call", output_to_operand_aliasing={{}: (8, {})} | custom-call | flops 18790481920 | bytes 49283072 | tf_op jit(solution)/shard_map/product/pallas_call | solution.py:186
  (79 shorter events, 20.2 us)
Async XLA Ops:
  6.5 129.3 %all-gather.3.cloned.1.call-start = ((), (), s32[]{:S(2)}) async-start(), calls=%async_computation | async-start | bytes 9437184 | tf_op jit(solution)/shard_map/all_gather | solution.py:278
  7.8 1.8 copy-start.4
  9.0 182.8 %all-gather.5.cloned.1.call-start = ((), (), s32[]{:S(2)}) async-start(), calls=%async_computation.1 | async-start | bytes 5898240 | tf_op jit(solution)/shard_map/all_gather | solution.py:278
  10.7 4.7 %copy-start.8 = (f32[2]{0:T(128)S(1)}, f32[2]{0:T(128)}, u32[]{:S(2)}) copy-start(f32[2]{0:T(128)} %param.7) | copy-start | bytes 28
  10.7 5.2 %copy-start.9 = (f32[2]{0:T(128)S(1)}, f32[2]{0:T(128)}, u32[]{:S(2)}) copy-start(f32[2]{0:T(128)} %param.6) | copy-start | bytes 28
  10.7 13.2 %copy-start.7 = (s32[1024]{0:T(1024)S(1)}, s32[1024]{0:T(1024)}, u32[]{:S(2)}) copy-start(s32[1024]{0:T(1024)} %param.5) | copy-start | bytes 12292
  11.5 17.2 %collective-permute-start = (bf16[128,1792]{1,0:T(8,128)(2,1)}, bf16[128,1792]{1,0:T(8,128)(2,1)S(1)}, u32[]{:S(2)}, u32[]{:S(2)}) collective-permute-start(bf16[128,1792]{1,0:T(8,128)(2,1)} %pad_maximum_fusion.8), channel_id=1, source_target_pairs={{0,1},{1,0},{2,3},{3,2},{4,5},{5,4},{6,7},{7,6},{8,9},{9,8},{10,11... | collective-permute-start | bytes 1376264 | tf_op jit(solution)/shard_map/ppermute | solution.py:219
  13.8 14.9 %collective-permute-start.1 = (bf16[128,1792]{1,0:T(8,128)(2,1)}, bf16[128,1792]{1,0:T(8,128)(2,1)S(1)}, u32[]{:S(2)}, u32[]{:S(2)}) collective-permute-start(bf16[128,1792]{1,0:T(8,128)(2,1)} %pad_maximum_fusion.9), channel_id=1, source_target_pairs={{0,2},{1,3},{2,0},{3,1},{4,6},{5,7},{6,4},{7,5},{8,10},{9,11},{10,... | collective-permute-start | bytes 1376264 | tf_op jit(solution)/shard_map/ppermute | solution.py:219
  28.1 12.7 %collective-permute-start.2 = (bf16[128,1792]{1,0:T(8,128)(2,1)S(1)}, bf16[128,1792]{1,0:T(8,128)(2,1)S(1)}, u32[]{:S(2)}, u32[]{:S(2)}) collective-permute-start(bf16[128,1792]{1,0:T(8,128)(2,1)S(1)} %pad_maximum_fusion.10), channel_id=1, source_target_pairs={{0,3},{1,2},{2,1},{3,0},{4,7},{5,6},{6,5},{7,4},{8,11},{9,10},{10,... | collective-permute-start | bytes 1376264 | tf_op jit(solution)/shard_map/ppermute | solution.py:219
  41.2 39.9 %collective-permute-start.3 = (bf16[128,1792]{1,0:T(8,128)(2,1)S(1)}, bf16[128,1792]{1,0:T(8,128)(2,1)S(1)}, u32[]{:S(2)}, u32[]{:S(2)}) collective-permute-start(bf16[128,1792]{1,0:T(8,128)(2,1)S(1)} %get-tuple-element.32), channel_id=1, source_target_pairs={{0,8},{4,12},{8,0},{12,4},{16,24},{20,28},{24,16},{28,20},{1,9},{5... | collective-permute-start | bytes 1376264 | tf_op jit(solution)/shard_map/ppermute | solution.py:219
  41.7 44.1 %collective-permute-start.4 = (bf16[128,1792]{1,0:T(8,128)(2,1)S(1)}, bf16[128,1792]{1,0:T(8,128)(2,1)S(1)}, u32[]{:S(2)}, u32[]{:S(2)}) collective-permute-start(bf16[128,1792]{1,0:T(8,128)(2,1)S(1)} %get-tuple-element.31), channel_id=1, source_target_pairs={{0,16},{4,20},{8,24},{12,28},{16,0},{20,4},{24,8},{28,12},{1,17},{... | collective-permute-start | bytes 1376264 | tf_op jit(solution)/shard_map/ppermute | solution.py:219
  44.3 82.3 %collective-permute-start.5 = (bf16[128,1792]{1,0:T(8,128)(2,1)S(1)}, bf16[128,1792]{1,0:T(8,128)(2,1)S(1)}, u32[]{:S(2)}, u32[]{:S(2)}) collective-permute-start(bf16[128,1792]{1,0:T(8,128)(2,1)S(1)} %get-tuple-element.30), channel_id=1, source_target_pairs={{0,24},{4,28},{8,16},{12,20},{16,8},{20,12},{24,0},{28,4},{1,25},{... | collective-permute-start | bytes 1376264 | tf_op jit(solution)/shard_map/ppermute | solution.py:219
  127.0 2.5 collective-permute-start.6
  135.8 5.8 %copy-start = (bf16[896,1024]{1,0:T(8,128)(2,1)S(1)}, bf16[896,1024]{1,0:T(8,128)(2,1)}, u32[]{:S(2)}) copy-start(bf16[896,1024]{1,0:T(8,128)(2,1)} %whiten_rows.1.refs_0_) | copy-start | bytes 5505028
  141.3 30.9 %collective-permute-start.11 = (bf16[1024,2048]{1,0:T(8,128)(2,1)}, bf16[1024,2048]{1,0:T(8,128)(2,1)S(1)}, u32[]{:S(2)}, u32[]{:S(2)}) collective-permute-start(bf16[1024,2048]{1,0:T(8,128)(2,1)} %whiten_columns.2.refs_1_.refs_3_.refs_2_), channel_id=1, source_target_pairs={{0,4},{4,0},{8,12},{12,8},{16,20},{20,16},{24,28},{28,24},{1,5},{5... | collective-permute-start | bytes 12582920 | tf_op jit(solution)/shard_map/ppermute | solution.py:219
  142.7 22.5 %collective-permute-start.7 = (bf16[448,1024]{1,0:T(8,128)(2,1)S(1)}, bf16[448,1024]{1,0:T(8,128)(2,1)S(1)}, u32[]{:S(2)}, u32[]{:S(2)}) collective-permute-start(bf16[448,1024]{1,0:T(8,128)(2,1)S(1)} %get-tuple-element.26), channel_id=1, source_target_pairs={{0,1},{1,0},{2,3},{3,2},{4,5},{5,4},{6,7},{7,6},{8,9},{9,8},{10,11... | collective-permute-start | bytes 2752520 | tf_op jit(solution)/shard_map/ppermute | solution.py:219
  143.4 22.5 %collective-permute-start.8 = (bf16[448,1024]{1,0:T(8,128)(2,1)}, bf16[448,1024]{1,0:T(8,128)(2,1)S(1)}, u32[]{:S(2)}, u32[]{:S(2)}) collective-permute-start(bf16[448,1024]{1,0:T(8,128)(2,1)} %get-tuple-element.25), channel_id=1, source_target_pairs={{0,2},{1,3},{2,0},{3,1},{4,6},{5,7},{6,4},{7,5},{8,10},{9,11},{10,... | collective-permute-start | bytes 2752520 | tf_op jit(solution)/shard_map/ppermute | solution.py:219
  165.3 4.9 %copy-start.2 = (bf16[448,1024]{1,0:T(8,128)(2,1)}, bf16[448,1024]{1,0:T(8,128)(2,1)S(1)}, u32[]{:S(2)}) copy-start(bf16[448,1024]{1,0:T(8,128)(2,1)S(1)} %collective-permute-done.7.refs_1_) | copy-start | bytes 2752516
  165.9 2.9 %copy-start.3 = (bf16[448,1024]{1,0:T(8,128)(2,1)}, bf16[448,1024]{1,0:T(8,128)(2,1)S(1)}, u32[]{:S(2)}) copy-start(bf16[448,1024]{1,0:T(8,128)(2,1)S(1)} %collective-permute-done.8.refs_2_) | copy-start | bytes 2752516
  168.8 41.5 %collective-permute-start.10 = (bf16[896,1024]{1,0:T(8,128)(2,1)}, bf16[896,1024]{1,0:T(8,128)(2,1)}, u32[]{:S(2)}, u32[]{:S(2)}) collective-permute-start(bf16[896,1024]{1,0:T(8,128)(2,1)} %pad_maximum_fusion.4), channel_id=1, source_target_pairs={{0,1},{1,0},{2,3},{3,2},{4,5},{5,4},{6,7},{7,6},{8,9},{9,8},{10,11... | collective-permute-start | bytes 5505032 | tf_op jit(solution)/shard_map/ppermute | solution.py:219
  171.5 41.1 %collective-permute-start.9 = (bf16[896,1024]{1,0:T(8,128)(2,1)}, bf16[896,1024]{1,0:T(8,128)(2,1)S(1)}, u32[]{:S(2)}, u32[]{:S(2)}) collective-permute-start(bf16[896,1024]{1,0:T(8,128)(2,1)} %pad_maximum_fusion.3), channel_id=1, source_target_pairs={{0,2},{1,3},{2,0},{3,1},{4,6},{5,7},{6,4},{7,5},{8,10},{9,11},{10,... | collective-permute-start | bytes 5505032 | tf_op jit(solution)/shard_map/ppermute | solution.py:219
  172.2 2.0 copy-start.1
  196.4 39.2 %collective-permute-start.12 = (bf16[1024,1280]{1,0:T(8,128)(2,1)}, bf16[1024,1280]{1,0:T(8,128)(2,1)S(1)}, u32[]{:S(2)}, u32[]{:S(2)}) collective-permute-start(bf16[1024,1280]{1,0:T(8,128)(2,1)} %whiten_columns.3.refs_5_), channel_id=1, source_target_pairs={{0,4},{4,0},{8,12},{12,8},{16,20},{20,16},{24,28},{28,24},{1,5},{5... | collective-permute-start | bytes 7864328 | tf_op jit(solution)/shard_map/ppermute | solution.py:219
  235.6 1.5 copy-start.6
  (1 other events, 1.3 us)
Sparse Core Ops, SparseCore 0:
  9.1 116.9 all-gather.2
  127.8 57.8 all-gather.4
where the time goes:
time: 279 us; the launch traced here: 274 us
  waiting for transfers between devices  123 us (44%)
  Pallas kernels  93.4 us (33%)
  between operations  21.2 us (8%)
  local copies, waits for them, and re-layouts  12.9 us (5%)
  other arithmetic  12.9 us (5%)
  starting transfers between devices  11 us (4%)
    ppermute x13, waiting for transfers between devices, swapped(): lax.ppermute(value, axis, [(i, i ^ distance) for i in range(lax.axis_size...  123 us
    pallas_call x4, Pallas kernels, product(): pl.pallas_call(functools.partial(product_kernel, parts, wides, pairs, sub...  78.5 us
    ppermute x13, starting transfers between devices, swapped(): lax.ppermute(value, axis, [(i, i ^ distance) for i in range(lax.axis_size...  10.9 us
    pallas_call x2, Pallas kernels, whiten_columns(): pl.pallas_call(functools.partial(whiten_columns_kernel, rows), grid_spec=...  10.1 us
  transfers between devices with their start and end apart: 15, of which 9 were waited for; matrix products, arithmetic and copies ran while one was open for 7% of the time, Pallas kernels for 23%

commit v1 on v0

--- a/solution.py
+++ b/solution.py
@@ -309,12 +309,11 @@
     out, raw = lax.optimization_barrier((out, raws[1][1]))
     raws[1] = (raws[1][0], raw)
     more = columns_of(1, own[2])
-    late = groups[-1]
-    out, mine = lax.optimization_barrier((out, more[0][2]))
-    more = ((True, more[0][1], mine), more[1])
-    out = product(place, late, [own, others], [(i, j) for j in range(2) for i in range(len(late))], out, shape, sub)
-    every = early + late
-    return product(place, every, more, [(i, j) for j in range(2) for i in range(len(every))], out, shape, sub)
+    pairs = [(i, j) for j in range(2) for i in range(len(early))]
+    out = product(place, early, more, pairs, out, shape, sub)
+    late, every = groups[-1], [own, others, *more]
+    pairs = [(i, j) for j in range(len(every)) for i in range(len(late))]
+    return product(place, late, every, pairs, out, shape, sub)
 
 
 def solution(mesh):

time: 279 us -> 290 us (1.039)
  the two profiles are of different devices: /device:TPU:8 before, /device:TPU:0 now
where the time goes in v1:
time: 290 us; the launch traced here: 286 us
  waiting for transfers between devices  129 us (44%)
  Pallas kernels  93.6 us (32%)
  between operations  21.2 us (7%)
  starting transfers between devices  15.5 us (5%)
  local copies, waits for them, and re-layouts  14 us (5%)
  other arithmetic  12.6 us (4%)
    ppermute x13, waiting for transfers between devices, swapped(): lax.ppermute(value, axis, [(i, i ^ distance) for i in range(lax.axis_size...  106 us
    pallas_call x4, Pallas kernels, product(): pl.pallas_call(functools.partial(product_kernel, parts, wides, pairs, sub...  79.1 us
    all_gather x2, waiting for transfers between devices, local(): raws.append((at, lax.all_gather(mine, 'row', axis=0, tiled=True)))  22.3 us
    ppermute x13, starting transfers between devices, swapped(): lax.ppermute(value, axis, [(i, i ^ distance) for i in range(lax.axis_size...  15.4 us
    pallas_call x2, Pallas kernels, whiten_columns(): pl.pallas_call(functools.partial(whiten_columns_kernel, rows), grid_spec=...  9.75 us
    unnamed x26, local copies, waits for them, and re-layouts  6.49 us
  transfers between devices with their start and end apart: 15, of which 11 were waited for; matrix products, arithmetic and copies ran while one was open for 6% of the time, Pallas kernels for 19%

profile of v1, /device:TPU:0, one launch (start us, length us, event | category | flops | bytes accessed | tf_op | source)
XLA Modules:
  0.0 285.5 jit_solution(14872815021085014026)
XLA Ops:
  11.5 2.9 %collective-permute-start = (bf16[128,1792]{1,0:T(8,128)(2,1)}, bf16[128,1792]{1,0:T(8,128)(2,1)S(1)}, u32[]{:S(2)}, u32[]{:S(2)}) collective-permute-start(bf16[128,1792]{1,0:T(8,128)(2,1)} %pad_maximum_fusion.8), channel_id=1, source_target_pairs={{0,1},{1,0},{2,3},{3,2},{4,5},{5,4},{6,7},{7,6},{8,9},{9,8},{10,11... | collective-permute-start | bytes 1376264 | tf_op jit(solution)/shard_map/ppermute | solution.py:219
  15.3 1.5 collective-permute-start.1
  29.8 12.5 %collective-permute-done.2 = bf16[128,1792]{1,0:T(8,128)(2,1)S(1)} collective-permute-done((bf16[128,1792]{1,0:T(8,128)(2,1)S(1)}, bf16[128,1792]{1,0:T(8,128)(2,1)S(1)}, u32[]{:S(2)}, u32[]{:S(2)}) %collective-permute-start.2) | collective-permute-done | bytes 458784 | tf_op jit(solution)/shard_map/ppermute | solution.py:219
  42.6 1.6 collective-permute-start.3
  44.3 2.6 collective-permute-start.4
  47.2 37.7 %collective-permute-done.3 = bf16[128,1792]{1,0:T(8,128)(2,1)S(1)} collective-permute-done((bf16[128,1792]{1,0:T(8,128)(2,1)S(1)}, bf16[128,1792]{1,0:T(8,128)(2,1)S(1)}, u32[]{:S(2)}, u32[]{:S(2)}) %collective-permute-start.3) | collective-permute-done | bytes 458784 | tf_op jit(solution)/shard_map/ppermute | solution.py:219
  84.9 7.4 %collective-permute-done.4 = bf16[128,1792]{1,0:T(8,128)(2,1)S(1)} collective-permute-done((bf16[128,1792]{1,0:T(8,128)(2,1)S(1)}, bf16[128,1792]{1,0:T(8,128)(2,1)S(1)}, u32[]{:S(2)}, u32[]{:S(2)}) %collective-permute-start.4) | collective-permute-done | bytes 458784 | tf_op jit(solution)/shard_map/ppermute | solution.py:219
  92.3 14.1 %collective-permute-done.5 = bf16[128,1792]{1,0:T(8,128)(2,1)S(1)} collective-permute-done((bf16[128,1792]{1,0:T(8,128)(2,1)S(1)}, bf16[128,1792]{1,0:T(8,128)(2,1)S(1)}, u32[]{:S(2)}, u32[]{:S(2)}) %collective-permute-start.5) | collective-permute-done | bytes 458784 | tf_op jit(solution)/shard_map/ppermute | solution.py:219
  110.8 4.8 %whiten_rows.1.refs_0_ = bf16[896,1024]{1,0:T(8,128)(2,1)} custom-call(s32[10]{0:T(128)} %stack.80.place, bf16[8,128,896]{2,1,0:T(8,128)(2,1)} %pad_maximum_fusion.2.raw, bf16[8,144,256]{2,1,0:T(8,128)(2,1)} %pad_maximum_fusion.7.matrix, f32[8,128,8]{2,1,0:T(8,128)} %pad.9.gains), custom_call_target="tpu_custom_call" | custom-call | flops 2113929216 | bytes 3670016 | tf_op jit(solution)/shard_map/whiten_rows/pallas_call | solution.py:114
  115.6 17.3 %all-gather.3.cloned.1.call-done.raw = bf16[1024,4096]{1,0:T(8,128)(2,1)} async-done(((bf16[128,4096]{1,0:T(8,128)(2,1)}), bf16[1024,4096]{1,0:T(8,128)(2,1)}) %all-gather.3.cloned.1.call-update) | async-done | bytes 8388624 | tf_op jit(solution)/shard_map/all_gather | solution.py:278
  132.9 5.4 %whiten_columns.2.refs_1_.refs_3_.refs_2_ = bf16[1024,2048]{1,0:T(8,128)(2,1)} custom-call(s32[1]{0:T(128)} %bitcast.core, bf16[1024,4096]{1,0:T(8,128)(2,1)} %all-gather.3.cloned.1.call-done.raw, bf16[8,144,256]{2,1,0:T(8,128)(2,1)} %pad_maximum_fusion.7.matrix, f32[8,128,8]{2,1,0:T(8,128)} %pad.9.gains), custom_call_target="tpu_custom_call" | custom-call | flops 4831838208 | bytes 8388608 | tf_op jit(solution)/shard_map/whiten_columns/pallas_call | solution.py:79
  139.6 1.5 collective-permute-start.7
  142.5 9.2 %product.4.refs_5_ = f32[3328,6656]{1,0:T(8,128)} custom-call(s32[10]{0:T(128)} %stack.80.place, bf16[896,1024]{1,0:T(8,128)(2,1)} %whiten_rows.1.refs_0_, bf16[1024,2048]{1,0:T(8,128)(2,1)} %whiten_columns.2.refs_1_.refs_3_.refs_2_), custom_call_target="tpu_custom_call" | custom-call | flops 3758096384 | bytes 13369344 | tf_op jit(solution)/shard_map/product/pallas_call | solution.py:186
  151.8 10.4 %collective-permute-done.7.refs_1_ = bf16[448,1024]{1,0:T(8,128)(2,1)S(1)} collective-permute-done((bf16[448,1024]{1,0:T(8,128)(2,1)S(1)}, bf16[448,1024]{1,0:T(8,128)(2,1)S(1)}, u32[]{:S(2)}, u32[]{:S(2)}) %collective-permute-start.7) | collective-permute-done | bytes 917536 | tf_op jit(solution)/shard_map/ppermute | solution.py:219
  164.4 2.0 copy-done.1
  166.4 17.6 %product.5.refs_5_ = f32[3328,6656]{1,0:T(8,128)} custom-call(s32[10]{0:T(128)} %stack.80.place, bf16[896,1024]{1,0:T(8,128)(2,1)} %whiten_rows.1.refs_0_, bf16[448,1024]{1,0:T(8,128)(2,1)} %copy-done.3, bf16[448,1024]{1,0:T(8,128)(2,1)} %copy-done.5, bf16[1024,2048]{1,0:T(8,128)(2,1)} %whiten_columns.2.refs_1_.refs_3_.refs_2_, ...), custom_call_target="tpu_custom_call", output_to_operand_aliasing={{}: (6, {})} | custom-call | flops 11274289152 | bytes 34078720 | tf_op jit(solution)/shard_map/product/pallas_call | solution.py:186
  184.0 4.9 %all-gather.5.cloned.1.call-done.raw = bf16[1024,2560]{1,0:T(8,128)(2,1)} async-done(((bf16[128,2560]{1,0:T(8,128)(2,1)}), bf16[1024,2560]{1,0:T(8,128)(2,1)}) %all-gather.5.cloned.1.call-update) | async-done | bytes 5242896 | tf_op jit(solution)/shard_map/all_gather | solution.py:278
  189.0 4.4 %whiten_columns.3.refs_3_.refs_4_ = bf16[1024,1280]{1,0:T(8,128)(2,1)} custom-call(s32[1]{0:T(128)} %bitcast.core, bf16[1024,2560]{1,0:T(8,128)(2,1)} %all-gather.5.cloned.1.call-done.raw, bf16[8,144,256]{2,1,0:T(8,128)(2,1)} %pad_maximum_fusion.7.matrix, f32[8,128,8]{2,1,0:T(8,128)} %pad.9.gains), custom_call_target="tpu_custom_call" | custom-call | flops 3019898880 | bytes 5242880 | tf_op jit(solution)/shard_map/whiten_columns/pallas_call | solution.py:79
  193.7 2.6 pad_maximum_fusion.4
  196.2 1.5 pad_maximum_fusion.3
  200.7 1.6 copy-done.2
  202.2 16.5 %product.6.refs_6_ = f32[3328,6656]{1,0:T(8,128)} custom-call(s32[10]{0:T(128)} %stack.80.place, bf16[896,1024]{1,0:T(8,128)(2,1)} %whiten_rows.1.refs_0_, bf16[448,1024]{1,0:T(8,128)(2,1)} %copy-done.3, bf16[448,1024]{1,0:T(8,128)(2,1)} %copy-done.5, bf16[1024,1280]{1,0:T(8,128)(2,1)} %whiten_columns.3.refs_3_.refs_4_, ...), custom_call_target="tpu_custom_call", output_to_operand_aliasing={{}: (6, {})} | custom-call | flops 9395240960 | bytes 27262976 | tf_op jit(solution)/shard_map/product/pallas_call | solution.py:186
  218.7 21.4 %collective-permute-done.10.refs_1_ = bf16[896,1024]{1,0:T(8,128)(2,1)S(1)} collective-permute-done((bf16[896,1024]{1,0:T(8,128)(2,1)}, bf16[896,1024]{1,0:T(8,128)(2,1)S(1)}, u32[]{:S(2)}, u32[]{:S(2)}) %collective-permute-start.10) | collective-permute-done | bytes 1835040 | tf_op jit(solution)/shard_map/ppermute | solution.py:219
  242.7 35.8 %product.7 = f32[3328,6656]{1,0:T(8,128)} custom-call(s32[10]{0:T(128)} %stack.80.place, bf16[896,1024]{1,0:T(8,128)(2,1)} %copy-done.9, bf16[896,1024]{1,0:T(8,128)(2,1)} %copy-done.8, bf16[1024,2048]{1,0:T(8,128)(2,1)} %whiten_columns.2.refs_1_.refs_3_.refs_2_, bf16[1024,2048]{1,0:T(8,128)(2,1)} %copy-done.1, ...), custom_call_target="tpu_custom_call", output_to_operand_aliasing={{}: (7, {})} | custom-call | flops 24427626496 | bytes 65011712 | tf_op jit(solution)/shard_map/product/pallas_call | solution.py:186
  (85 shorter events, 27.2 us)
Async XLA Ops:
  6.5 126.4 %all-gather.3.cloned.1.call-start = ((), (), s32[]{:S(2)}) async-start(), calls=%async_computation | async-start | bytes 9437184 | tf_op jit(solution)/shard_map/all_gather | solution.py:278
  7.8 1.8 copy-start.7
  9.0 180.0 %all-gather.5.cloned.1.call-start = ((), (), s32[]{:S(2)}) async-start(), calls=%async_computation.1 | async-start | bytes 5898240 | tf_op jit(solution)/shard_map/all_gather | solution.py:278
  10.7 6.1 %copy-start.11 = (f32[2]{0:T(128)S(1)}, f32[2]{0:T(128)}, u32[]{:S(2)}) copy-start(f32[2]{0:T(128)} %param.7) | copy-start | bytes 28
  10.7 6.7 %copy-start.12 = (f32[2]{0:T(128)S(1)}, f32[2]{0:T(128)}, u32[]{:S(2)}) copy-start(f32[2]{0:T(128)} %param.6) | copy-start | bytes 28
  10.7 14.7 %copy-start.10 = (s32[1024]{0:T(1024)S(1)}, s32[1024]{0:T(1024)}, u32[]{:S(2)}) copy-start(s32[1024]{0:T(1024)} %param.5) | copy-start | bytes 12292
  11.5 18.2 %collective-permute-start = (bf16[128,1792]{1,0:T(8,128)(2,1)}, bf16[128,1792]{1,0:T(8,128)(2,1)S(1)}, u32[]{:S(2)}, u32[]{:S(2)}) collective-permute-start(bf16[128,1792]{1,0:T(8,128)(2,1)} %pad_maximum_fusion.8), channel_id=1, source_target_pairs={{0,1},{1,0},{2,3},{3,2},{4,5},{5,4},{6,7},{7,6},{8,9},{9,8},{10,11... | collective-permute-start | bytes 1376264 | tf_op jit(solution)/shard_map/ppermute | solution.py:219
  15.3 14.5 %collective-permute-start.1 = (bf16[128,1792]{1,0:T(8,128)(2,1)}, bf16[128,1792]{1,0:T(8,128)(2,1)S(1)}, u32[]{:S(2)}, u32[]{:S(2)}) collective-permute-start(bf16[128,1792]{1,0:T(8,128)(2,1)} %pad_maximum_fusion.9), channel_id=1, source_target_pairs={{0,2},{1,3},{2,0},{3,1},{4,6},{5,7},{6,4},{7,5},{8,10},{9,11},{10,... | collective-permute-start | bytes 1376264 | tf_op jit(solution)/shard_map/ppermute | solution.py:219
  29.6 12.7 %collective-permute-start.2 = (bf16[128,1792]{1,0:T(8,128)(2,1)S(1)}, bf16[128,1792]{1,0:T(8,128)(2,1)S(1)}, u32[]{:S(2)}, u32[]{:S(2)}) collective-permute-start(bf16[128,1792]{1,0:T(8,128)(2,1)S(1)} %pad_maximum_fusion.10), channel_id=1, source_target_pairs={{0,3},{1,2},{2,1},{3,0},{4,7},{5,6},{6,5},{7,4},{8,11},{9,10},{10,... | collective-permute-start | bytes 1376264 | tf_op jit(solution)/shard_map/ppermute | solution.py:219
  42.6 42.3 %collective-permute-start.3 = (bf16[128,1792]{1,0:T(8,128)(2,1)S(1)}, bf16[128,1792]{1,0:T(8,128)(2,1)S(1)}, u32[]{:S(2)}, u32[]{:S(2)}) collective-permute-start(bf16[128,1792]{1,0:T(8,128)(2,1)S(1)} %get-tuple-element.28), channel_id=1, source_target_pairs={{0,8},{4,12},{8,0},{12,4},{16,24},{20,28},{24,16},{28,20},{1,9},{5... | collective-permute-start | bytes 1376264 | tf_op jit(solution)/shard_map/ppermute | solution.py:219
  44.3 48.0 %collective-permute-start.4 = (bf16[128,1792]{1,0:T(8,128)(2,1)S(1)}, bf16[128,1792]{1,0:T(8,128)(2,1)S(1)}, u32[]{:S(2)}, u32[]{:S(2)}) collective-permute-start(bf16[128,1792]{1,0:T(8,128)(2,1)S(1)} %get-tuple-element.27), channel_id=1, source_target_pairs={{0,16},{4,20},{8,24},{12,28},{16,0},{20,4},{24,8},{28,12},{1,17},{... | collective-permute-start | bytes 1376264 | tf_op jit(solution)/shard_map/ppermute | solution.py:219
  46.8 59.5 %collective-permute-start.5 = (bf16[128,1792]{1,0:T(8,128)(2,1)S(1)}, bf16[128,1792]{1,0:T(8,128)(2,1)S(1)}, u32[]{:S(2)}, u32[]{:S(2)}) collective-permute-start(bf16[128,1792]{1,0:T(8,128)(2,1)S(1)} %get-tuple-element.26), channel_id=1, source_target_pairs={{0,24},{4,28},{8,16},{12,20},{16,8},{20,12},{24,0},{28,4},{1,25},{... | collective-permute-start | bytes 1376264 | tf_op jit(solution)/shard_map/ppermute | solution.py:219
  106.9 2.5 collective-permute-start.6
  115.6 23.0 %copy-start = (bf16[896,1024]{1,0:T(8,128)(2,1)S(1)}, bf16[896,1024]{1,0:T(8,128)(2,1)}, u32[]{:S(2)}) copy-start(bf16[896,1024]{1,0:T(8,128)(2,1)} %whiten_rows.1.refs_0_) | copy-start | bytes 5505028
  138.3 25.2 %collective-permute-start.11 = (bf16[1024,2048]{1,0:T(8,128)(2,1)}, bf16[1024,2048]{1,0:T(8,128)(2,1)S(1)}, u32[]{:S(2)}, u32[]{:S(2)}) collective-permute-start(bf16[1024,2048]{1,0:T(8,128)(2,1)} %whiten_columns.2.refs_1_.refs_3_.refs_2_), channel_id=1, source_target_pairs={{0,4},{4,0},{8,12},{12,8},{16,20},{20,16},{24,28},{28,24},{1,5},{5... | collective-permute-start | bytes 12582920 | tf_op jit(solution)/shard_map/ppermute | solution.py:219
  139.6 22.5 %collective-permute-start.7 = (bf16[448,1024]{1,0:T(8,128)(2,1)S(1)}, bf16[448,1024]{1,0:T(8,128)(2,1)S(1)}, u32[]{:S(2)}, u32[]{:S(2)}) collective-permute-start(bf16[448,1024]{1,0:T(8,128)(2,1)S(1)} %get-tuple-element.22), channel_id=1, source_target_pairs={{0,1},{1,0},{2,3},{3,2},{4,5},{5,4},{6,7},{7,6},{8,9},{9,8},{10,11... | collective-permute-start | bytes 2752520 | tf_op jit(solution)/shard_map/ppermute | solution.py:219
  141.1 22.4 %collective-permute-start.8 = (bf16[448,1024]{1,0:T(8,128)(2,1)}, bf16[448,1024]{1,0:T(8,128)(2,1)S(1)}, u32[]{:S(2)}, u32[]{:S(2)}) collective-permute-start(bf16[448,1024]{1,0:T(8,128)(2,1)} %get-tuple-element.21), channel_id=1, source_target_pairs={{0,2},{1,3},{2,0},{3,1},{4,6},{5,7},{6,4},{7,5},{8,10},{9,11},{10,... | collective-permute-start | bytes 2752520 | tf_op jit(solution)/shard_map/ppermute | solution.py:219
  164.4 2.0 copy-start.1
  184.0 9.6 %copy-start.6 = (bf16[448,1024]{1,0:T(8,128)(2,1)S(1)}, bf16[448,1024]{1,0:T(8,128)(2,1)}, u32[]{:S(2)}) copy-start(bf16[448,1024]{1,0:T(8,128)(2,1)} %copy-done.5) | copy-start | bytes 2752516
  193.4 2.9 %copy-start.4 = (bf16[448,1024]{1,0:T(8,128)(2,1)S(1)}, bf16[448,1024]{1,0:T(8,128)(2,1)}, u32[]{:S(2)}) copy-start(bf16[448,1024]{1,0:T(8,128)(2,1)} %copy-done.3) | copy-start | bytes 2752516
  193.4 7.3 %collective-permute-start.12 = (bf16[1024,1280]{1,0:T(8,128)(2,1)}, bf16[1024,1280]{1,0:T(8,128)(2,1)S(1)}, u32[]{:S(2)}, u32[]{:S(2)}) collective-permute-start(bf16[1024,1280]{1,0:T(8,128)(2,1)} %whiten_columns.3.refs_3_.refs_4_), channel_id=1, source_target_pairs={{0,4},{4,0},{8,12},{12,8},{16,20},{20,16},{24,28},{28,24},{1,5},{5... | collective-permute-start | bytes 7864328 | tf_op jit(solution)/shard_map/ppermute | solution.py:219
  197.7 42.4 %collective-permute-start.10 = (bf16[896,1024]{1,0:T(8,128)(2,1)}, bf16[896,1024]{1,0:T(8,128)(2,1)S(1)}, u32[]{:S(2)}, u32[]{:S(2)}) collective-permute-start(bf16[896,1024]{1,0:T(8,128)(2,1)} %pad_maximum_fusion.4), channel_id=1, source_target_pairs={{0,1},{1,0},{2,3},{3,2},{4,5},{5,4},{6,7},{7,6},{8,9},{9,8},{10,11... | collective-permute-start | bytes 5505032 | tf_op jit(solution)/shard_map/ppermute | solution.py:219
  199.2 42.1 %collective-permute-start.9 = (bf16[896,1024]{1,0:T(8,128)(2,1)}, bf16[896,1024]{1,0:T(8,128)(2,1)S(1)}, u32[]{:S(2)}, u32[]{:S(2)}) collective-permute-start(bf16[896,1024]{1,0:T(8,128)(2,1)} %pad_maximum_fusion.3), channel_id=1, source_target_pairs={{0,2},{1,3},{2,0},{3,1},{4,6},{5,7},{6,4},{7,5},{8,10},{9,11},{10,... | collective-permute-start | bytes 5505032 | tf_op jit(solution)/shard_map/ppermute | solution.py:219
  200.7 1.6 copy-start.2
  (4 other events, 4.9 us)
Sparse Core Ops, SparseCore 0:
  9.1 123.7 all-gather.2
  134.5 54.4 all-gather.4
